TPU v7x, 128 devices: a whole 4x4x4 slice. The times are simulated.
128 devices in a mesh: tm: 16 (over z, x), chan: 8 (over y, core).
Axes of the slice: x: 4, y: 4, z: 4, core: 2. Of those that a mesh axis runs over, the one named last changes fastest.
Arguments:
- records: float32 [64, 16, 8, 16, 4096], P('tm', None, 'chan'), may hold values from -6 to 6
- band_gain: float32 [384], replicated, may hold values from 0.5 to 2
- pair_mask: int32 [128, 5], P(('tm', 'chan')), may hold values 0 or 1
Outputs:
- stacks: float32 [128, 5, 16, 16, 2, 384], P(('tm', 'chan'))
All inputs are finite; a program needn't handle non-finite values. No bound on the sum of `pair_mask` on one device may be relied on, other than what follows from the above.
Results may differ from a plain program's by a relative error of at most 0.0031.
Values may be sent and summed in bfloat16 or wider, within the bound.
A program may use at most 256 MiB of HBM per device.

v0:
```python
import jax
import jax.numpy as jnp
import ml_dtypes
import numpy as np
from jax import lax
from jax.experimental import pallas as pl
from jax.experimental.pallas import tpu as pltpu
from jax.sharding import PartitionSpec as P

L = 4096
F0 = 8
HW = 64
NB = 384
EXT = NB + 2 * HW
NTM = 16
NCHAN = 8
NBLK = NTM * NCHAN
BS = 16
WL = 4
ROWS = NTM * BS
MESH = pl.DeviceIdType.MESH
F32 = jnp.float32
BF16 = jnp.bfloat16
OWN, ABOVE, X1, X2, BELOW = range(5)


def bin_order():
    j = np.arange(EXT)
    return np.concatenate([j[j % 4 == 0], j[j % 4 == 2], j[j % 2 == 1]])


def dft_tables():
    order = bin_order()

    def parts(samples, bins):
        phase = (np.arange(samples)[:, None] * (F0 + bins)[None, :] % L) * (2 * np.pi / L)
        return np.cos(phase) / 64.0, -np.sin(phase) / 64.0

    quarter = EXT // 4
    even = []
    for r in range(2):
        even += parts(L // 4, order[r * quarter : (r + 1) * quarter])
    even = np.concatenate(even, axis=1)
    odd = np.concatenate(parts(L // 2, order[2 * quarter :]), axis=1)

    def split(table):
        high = table.astype(ml_dtypes.bfloat16)
        low = (table - high.astype(np.float64)).astype(ml_dtypes.bfloat16)
        return np.stack([high, low])

    return np.concatenate([split(even), split(odd)], axis=1)


def smoother_table():
    order = bin_order()
    lower = order - HW
    covered = (order[:, None] >= lower[None, :]) & (order[:, None] <= lower[None, :] + 2 * HW)
    return covered.astype(ml_dtypes.bfloat16)


def order_table():
    order = bin_order()
    return (order[:, None] == np.arange(NB)[None, :] + HW).astype(ml_dtypes.bfloat16)


def hann_row():
    n = np.arange(L)
    return (0.5 - 0.5 * np.cos(2 * np.pi * n / L)).astype(np.float32)[None, :]


def device_of(block):
    wrapped = lax.rem(block + NBLK, NBLK)
    return (wrapped // NCHAN, lax.rem(wrapped, NCHAN))


def kernel(
    rec,
    tab_hbm,
    smooth,
    perm,
    hann,
    gain,
    mask,
    out,
    xbuf,
    tab,
    fold,
    spec,
    pw,
    lev,
    wh,
    gperm,
    send,
    blocks,
    wide,
    acc,
    give,
    take,
    rec_sem,
    tab_sem,
    a2a_s,
    a2a_r,
    ring_s,
    ring_r,
    sib_s,
    sib_r,
    give_s,
    give_r,
    out_sem,
):
    t = lax.axis_index("tm")
    c = lax.axis_index("chan")
    block = t * NCHAN + c
    core = lax.rem(c, 2)
    before = device_of(block - 2)
    after = device_of(block + 2)
    sibling = (t, c + 1 - 2 * core)

    def rec_copy(w):
        slot = lax.rem(w, 2)
        return pltpu.make_async_copy(rec.at[w], xbuf.at[slot], rec_sem.at[slot])

    tab_copy = pltpu.make_async_copy(tab_hbm, tab, tab_sem)
    rec_copy(0).start()
    tab_copy.start()
    rec_copy(1).start()

    barrier = pltpu.get_barrier_semaphore()
    for d in range(1, NTM):
        pl.semaphore_signal(
            barrier, inc=1, device_id=(lax.rem(t + d, NTM), c), device_id_type=MESH
        )
    for peer in (before, after, sibling):
        pl.semaphore_signal(barrier, inc=1, device_id=peer, device_id_type=MESH)

    def clear(i, _):
        acc[i // 16, lax.rem(i, 16)] = jnp.zeros((2, BS, NB), F32)
        return 0

    lax.fori_loop(0, 80, clear, 0)

    rest = jnp.broadcast_to(gain[...], (16, NB))
    total = jnp.zeros((16, EXT), F32)
    for _ in range(3):
        piece = rest.astype(BF16)
        rest = rest - piece.astype(F32)
        total += lax.dot_general(
            piece, perm[...], (((1,), (1,)), ((), ())), preferred_element_type=F32
        )
    gperm[...] = total

    def a2a_copy(w, d):
        q = lax.rem(t + d, NTM)
        return pltpu.make_async_remote_copy(
            src_ref=send.at[w, pl.ds(pl.multiple_of(q * BS, BS), BS)],
            dst_ref=blocks.at[OWN, w, t],
            send_sem=a2a_s.at[w, d],
            recv_sem=a2a_r.at[w, d],
            device_id=(q, c),
            device_id_type=MESH,
        )

    def ring_copy(w, up):
        return pltpu.make_async_remote_copy(
            src_ref=blocks.at[OWN, w],
            dst_ref=blocks.at[ABOVE if up else BELOW, w],
            send_sem=ring_s.at[w, up],
            recv_sem=ring_r.at[w, up],
            device_id=before if up else after,
            device_id_type=MESH,
        )

    def sib_copy(w, source, slot):
        return pltpu.make_async_remote_copy(
            src_ref=blocks.at[source, w],
            dst_ref=blocks.at[slot, w],
            send_sem=sib_s.at[w, slot - X1],
            recv_sem=sib_r.at[w, slot - X1],
            device_id=sibling,
            device_id_type=MESH,
        )

    def widen(which, source, w):
        def one(i, _):
            wide[which, w, i] = blocks[source, w, i].astype(F32)
            return 0

        lax.fori_loop(0, NTM, one, 0)

    def spread(w):
        for d in range(1, NTM):
            a2a_copy(w, d).wait_recv()
        ring_copy(w, 1).start()
        ring_copy(w, 0).start()

        @pl.when(core == 1)
        def _():
            sib_copy(w, OWN, X1).start()

        widen(0, OWN, w)

    def transform(w, _):
        slot = lax.rem(w, 2)
        rec_copy(w).wait()

        def fold_rows(i, _):
            rows = pl.ds(pl.multiple_of(i * 16, 16), 16)
            low_rows = pl.ds(pl.multiple_of(ROWS + i * 16, 16), 16)

            def put(value, at):
                high = value.astype(BF16)
                fold[rows, at : at + 128] = high
                fold[low_rows, at : at + 128] = (value - high.astype(F32)).astype(BF16)

            for p in range(0, L // 4, 128):
                x0, x1, x2, x3 = (
                    xbuf[slot, rows, s + p : s + p + 128] * hann[:, s + p : s + p + 128]
                    for s in range(0, L, L // 4)
                )
                u, v = x0 + x2, x1 + x3
                put(u + v, p)
                put(u - v, L // 4 + p)
                put(x0 - x2, L // 2 + p)
                put(x1 - x3, 3 * L // 4 + p)
            return 0

        lax.fori_loop(0, ROWS // 16, fold_rows, 0)

        @pl.when(w + 2 < WL)
        def _():
            rec_copy(w + 2).start()

        @pl.when(w == 0)
        def _():
            tab_copy.wait()

        def product(at, length, trow, tcol, col):
            both = jnp.dot(
                fold[:, at : at + length],
                tab[0, trow : trow + length, tcol : tcol + 256],
                preferred_element_type=F32,
            )
            low = jnp.dot(
                fold[:ROWS, at : at + length],
                tab[1, trow : trow + length, tcol : tcol + 256],
                preferred_element_type=F32,
            )
            spec[:, col : col + 256] = both[:ROWS] + (both[ROWS:] + low)

        product(0, L // 4, 0, 0, 0)
        product(L // 4, L // 4, 0, 256, 256)
        product(L // 2, L // 2, L // 4, 0, 512)
        product(L // 2, L // 2, L // 4, 256, 768)

        def spectrum(rows):
            re = jnp.concatenate([spec[rows, 0:128], spec[rows, 256:384], spec[rows, 512:768]], 1)
            im = jnp.concatenate([spec[rows, 128:256], spec[rows, 384:512], spec[rows, 768:1024]], 1)
            return re, im

        def power_rows(i, _):
            rows = pl.ds(pl.multiple_of(i * 16, 16), 16)
            re, im = spectrum(rows)
            power = re * re + im * im
            high = power.astype(BF16)
            pw[rows] = high
            pw[pl.ds(pl.multiple_of(ROWS + i * 16, 16), 16)] = (power - high.astype(F32)).astype(BF16)
            return 0

        lax.fori_loop(0, ROWS // 16, power_rows, 0)
        lev[...] = jnp.dot(pw[...], smooth[...], preferred_element_type=F32)

        def white_rows(i, _):
            rows = pl.ds(pl.multiple_of(i * 16, 16), 16)
            low_rows = pl.ds(pl.multiple_of(ROWS + i * 16, 16), 16)
            level = (lev[rows] + lev[low_rows]) / (2 * HW + 1)
            factor = gperm[...] * lax.rsqrt(level + 1e-6)
            re, im = spectrum(rows)
            wh[rows] = (re * factor).astype(BF16)
            wh[low_rows] = (im * factor).astype(BF16)
            return 0

        lax.fori_loop(0, ROWS // 16, white_rows, 0)
        white = jnp.dot(wh[...], perm[...], preferred_element_type=F32)
        send[w, :, 0:NB] = white[:ROWS].astype(BF16)
        send[w, :, NB:] = white[ROWS:].astype(BF16)

        @pl.when(w == 0)
        def _():
            pl.semaphore_wait(barrier, NTM - 1 + 3)

        for d in range(1, NTM):
            a2a_copy(w, d).start()
        blocks[OWN, w, t] = send[w, pl.ds(pl.multiple_of(t * BS, BS), BS)]

        @pl.when(w > 0)
        def _():
            spread(w - 1)

        return 0

    lax.fori_loop(0, WL, transform, 0)

    def correlate(k, left, right, w):
        def bins(i, _):
            re_at = pl.ds(pl.multiple_of(i * 128, 128), 128)
            im_at = pl.ds(pl.multiple_of(NB + i * 128, 128), 128)
            for half in range(2):
                mine = range(half * 8, half * 8 + 8)
                start = tuple(acc[k, a, p, :, re_at] for a in mine for p in range(2))

                def window(n, sums):
                    cr = blocks[right, w, n, :, re_at].astype(F32)
                    ci = blocks[right, w, n, :, im_at].astype(F32)
                    new = []
                    for i, a in enumerate(mine):
                        ar = wide[left, w, n, a : a + 1, re_at]
                        ai = wide[left, w, n, a : a + 1, im_at]
                        new.append(sums[2 * i] + (ar * cr + ai * ci))
                        new.append(sums[2 * i + 1] + (ai * cr - ar * ci))
                    return tuple(new)

                sums = lax.fori_loop(0, NTM, window, start)
                for i, a in enumerate(mine):
                    for p in range(2):
                        acc[k, a, p, :, re_at] = sums[2 * i + p]
            return 0

        lax.fori_loop(0, NB // 128, bins, 0)

    def selfs(w, _):
        correlate(0, 0, OWN, w)
        return 0

    lax.fori_loop(0, WL - 1, selfs, 0)
    spread(WL - 1)
    correlate(0, 0, OWN, WL - 1)

    def give_copy(i):
        return pltpu.make_async_remote_copy(
            src_ref=give.at[i],
            dst_ref=take.at[i],
            send_sem=give_s.at[i],
            recv_sem=give_r.at[i],
            device_id=before,
            device_id_type=MESH,
        )

    def hand_over(i, k):
        def one(a, _):
            give[i, a] = acc[k, a].astype(BF16)
            return 0

        lax.fori_loop(0, BS, one, 0)
        give_copy(i).start()

    left3 = core
    right3 = X2 - core

    def partners(w, _):
        ring_copy(w, 1).wait_recv()

        @pl.when(core == 0)
        def _():
            sib_copy(w, ABOVE, X1).start()

        @pl.when(core == 1)
        def _():
            sib_copy(w, ABOVE, X2).start()

        ring_copy(w, 0).wait_recv()
        widen(1, BELOW, w)
        correlate(4, 1, ABOVE, w)

        @pl.when(w == WL - 1)
        def _():
            hand_over(0, 4)

        sib_copy(w, OWN, X1).wait_recv()

        @pl.when(core == 0)
        def _():
            sib_copy(w, OWN, X2).wait_recv()

        correlate(3, left3, right3, w)

        @pl.when((w == WL - 1) & (core == 1))
        def _():
            hand_over(1, 3)

        correlate(1, 0, X1, w)
        correlate(2, 0, ABOVE, w)
        return 0

    lax.fori_loop(0, WL, partners, 0)

    def out_copy(k):
        return pltpu.make_async_copy(acc.at[k], out.at[k], out_sem.at[k])

    def weight_of(k):
        inside = (block + k < NBLK).astype(F32)
        return mask[0, k].astype(F32) * inside * (1.0 / 64.0)

    def finish(k):
        weight = weight_of(k)

        def one(a, _):
            acc[k, a] = acc[k, a] * weight
            return 0

        lax.fori_loop(0, BS, one, 0)
        out_copy(k).start()

    def finish_taken(k, i):
        give_copy(i).wait_recv()
        weight = weight_of(k)

        def one(a, _):
            acc[k, a] = take[i, a].astype(F32) * weight
            return 0

        lax.fori_loop(0, BS, one, 0)
        out_copy(k).start()

    for k in range(3):
        finish(k)

    @pl.when(core == 0)
    def _():
        finish(3)

    finish_taken(4, 0)

    @pl.when(core == 1)
    def _():
        finish_taken(3, 1)

    def drain(w, _):
        for d in range(1, NTM):
            a2a_copy(w, d).wait_send()
        ring_copy(w, 1).wait_send()
        ring_copy(w, 0).wait_send()

        @pl.when(core == 0)
        def _():
            sib_copy(w, ABOVE, X1).wait_send()

        @pl.when(core == 1)
        def _():
            sib_copy(w, OWN, X1).wait_send()
            sib_copy(w, ABOVE, X2).wait_send()

        return 0

    lax.fori_loop(0, WL, drain, 0)
    give_copy(0).wait_send()

    @pl.when(core == 1)
    def _():
        give_copy(1).wait_send()

    for k in range(5):
        out_copy(k).wait()


def body(records, band_gain, pair_mask):
    rec = records.reshape(WL, ROWS, L)
    any_space = pl.BlockSpec(memory_space=pl.ANY)
    vmem = pl.BlockSpec(memory_space=pltpu.VMEM)
    smem = pl.BlockSpec(memory_space=pltpu.SMEM)
    dma = pltpu.SemaphoreType.DMA
    sums = pl.pallas_call(
        kernel,
        out_shape=jax.ShapeDtypeStruct((5, BS, 2, BS, NB), F32),
        in_specs=[any_space, any_space, vmem, vmem, vmem, vmem, smem],
        out_specs=any_space,
        scratch_shapes=[
            pltpu.VMEM((2, ROWS, L), F32),
            pltpu.VMEM((2, 3 * L // 4, 512), BF16),
            pltpu.VMEM((2 * ROWS, L), BF16),
            pltpu.VMEM((ROWS, 2 * EXT), F32),
            pltpu.VMEM((2 * ROWS, EXT), BF16),
            pltpu.VMEM((2 * ROWS, EXT), F32),
            pltpu.VMEM((2 * ROWS, EXT), BF16),
            pltpu.VMEM((16, EXT), F32),
            pltpu.VMEM((WL, ROWS, 2 * NB), BF16),
            pltpu.VMEM((5, WL, NTM, BS, 2 * NB), BF16),
            pltpu.VMEM((2, WL, NTM, BS, 2 * NB), F32),
            pltpu.VMEM((5, BS, 2, BS, NB), F32),
            pltpu.VMEM((2, BS, 2, BS, NB), BF16),
            pltpu.VMEM((2, BS, 2, BS, NB), BF16),
            dma((2,)),
            dma,
            dma((WL, NTM)),
            dma((WL, NTM)),
            dma((WL, 2)),
            dma((WL, 2)),
            dma((WL, 2)),
            dma((WL, 2)),
            dma((2,)),
            dma((2,)),
            dma((5,)),
        ],
        compiler_params=pltpu.CompilerParams(
            collective_id=0, has_side_effects=True, vmem_limit_bytes=58 << 20
        ),
        cost_estimate=pl.CostEstimate(
            flops=10**10, bytes_accessed=30 * 10**6, transcendentals=10**6
        ),
    )(
        rec,
        jnp.asarray(dft_tables()),
        jnp.asarray(smoother_table()),
        jnp.asarray(order_table()),
        jnp.asarray(hann_row()),
        band_gain[None, :],
        pair_mask,
    )
    return sums.transpose(0, 1, 3, 2, 4)[None]


def solution(mesh):
    placed = (P("tm", None, "chan", None, None), P(), P(("tm", "chan"), None))
    return jax.shard_map(
        body,
        mesh=mesh,
        in_specs=placed,
        out_specs=P(("tm", "chan"), None, None, None, None, None),
        check_vma=False,
    )
```

profile of v0, /device:TPU:63, one launch (start us, length us, event | category | flops | bytes accessed | tf_op | source)
XLA Modules:
  0.0 123.4 jit_solution(524913016266644841)
XLA Ops:
  0.0 1.2 %broadcast_in_dim.6.gain = f32[1,384]{1,0:T(1,128)} reshape(f32[384]{0:T(512)} %param.8) | data formatting | bytes 3072 | tf_op jit(solution)/shard_map/broadcast_in_dim | solution.py:515
  1.2 116.0 %shard_map.73 = f32[5,16,2,16,384]{4,3,2,1,0:T(8,128)} custom-call(f32[4,256,4096]{2,1,0:T(8,128)} %bitcast.5, bf16[2,3072,512]{2,1,0:T(8,128)(2,1)} %constant.8.clone.tab_hbm, bf16[512,512]{1,0:T(8,128)(2,1)} %constant.9.clone.smooth, bf16[512,384]{1,0:T(8,128)(2,1)} %constant.10.clone.perm, f32[1,4096]{1,0:T(1,128)} %constant.11.clone.hann, ...), custom_call_target="tpu_custom_call" | custom-call | flops 10000000000 | bytes 30000000 | tf_op jit(solution)/shard_map/pallas_call | solution.py:471
  117.2 6.2 %copy.8 = f32[1,5,16,16,2,384]{5,4,3,2,1,0:T(2,128)} copy(f32[1,5,16,16,2,384]{5,3,4,2,1,0:T(8,128)} %bitcast.4) | data formatting | bytes 7864320 | tf_op jit(solution)/shard_map/broadcast_in_dim | solution.py:518
where the time goes:
time: 124 us; the launch traced here: 123 us
  Pallas kernels  116 us (94%)
  local copies, waits for them, and re-layouts  7.4 us (6%)
    pallas_call x1, Pallas kernels, body(): pl.pallas_call(kernel, out_shape=jax.ShapeDtypeStruct((5, BS, 2, BS, NB),...  116 us
    broadcast_in_dim x1, local copies, waits for them, and re-layouts, body(): return sums.transpose(0, 1, 3, 2, 4)[None]  6.16 us

commit v1 on v0

--- a/solution.py
+++ b/solution.py
@@ -100,6 +100,8 @@
     tab_sem,
     a2a_s,
     a2a_r,
+    dup_s,
+    dup_r,
     ring_s,
     ring_r,
     sib_s,
@@ -115,6 +117,11 @@
     before = device_of(block - 2)
     after = device_of(block + 2)
     sibling = (t, c + 1 - 2 * core)
+    first = c < 2
+    last = c >= NCHAN - 2
+    shift = jnp.where(first, 1, -1)
+    round_corner = lax.rem(c + 6 * shift + NCHAN, NCHAN)
+    dup_slot = jnp.where(first, ABOVE, BELOW)
 
     def rec_copy(w):
         slot = lax.rem(w, 2)
@@ -130,8 +137,22 @@
         pl.semaphore_signal(
             barrier, inc=1, device_id=(lax.rem(t + d, NTM), c), device_id_type=MESH
         )
-    for peer in (before, after, sibling):
-        pl.semaphore_signal(barrier, inc=1, device_id=peer, device_id_type=MESH)
+    pl.semaphore_signal(barrier, inc=1, device_id=sibling, device_id_type=MESH)
+
+    @pl.when(jnp.logical_not(first))
+    def _():
+        pl.semaphore_signal(barrier, inc=1, device_id=before, device_id_type=MESH)
+
+    @pl.when(jnp.logical_not(last))
+    def _():
+        pl.semaphore_signal(barrier, inc=1, device_id=after, device_id_type=MESH)
+
+    @pl.when(first | last)
+    def _():
+        for d in range(NTM):
+            pl.semaphore_signal(
+                barrier, inc=1, device_id=(lax.rem(t + d, NTM), round_corner), device_id_type=MESH
+            )
 
     def clear(i, _):
         acc[i // 16, lax.rem(i, 16)] = jnp.zeros((2, BS, NB), F32)
@@ -139,7 +160,7 @@
 
     lax.fori_loop(0, 80, clear, 0)
 
-    rest = jnp.broadcast_to(gain[...], (16, NB))
+    rest = jnp.broadcast_to(gain[...].reshape(1, NB), (16, NB))
     total = jnp.zeros((16, EXT), F32)
     for _ in range(3):
         piece = rest.astype(BF16)
@@ -160,44 +181,69 @@
             device_id_type=MESH,
         )
 
-    def ring_copy(w, up):
+    def dup_copy(w, d):
+        r = lax.rem(t + d, NTM)
+        q = lax.rem(r + shift + NTM, NTM)
         return pltpu.make_async_remote_copy(
-            src_ref=blocks.at[OWN, w],
-            dst_ref=blocks.at[ABOVE if up else BELOW, w],
-            send_sem=ring_s.at[w, up],
-            recv_sem=ring_r.at[w, up],
+            src_ref=send.at[w, pl.ds(pl.multiple_of(q * BS, BS), BS)],
+            dst_ref=blocks.at[dup_slot, w, t],
+            send_sem=dup_s.at[w, d],
+            recv_sem=dup_r.at[w, d],
+            device_id=(r, round_corner),
+            device_id_type=MESH,
+        )
+
+    def bins_of(ref, slot, w, f):
+        return ref.at[slot, w, :, :, pl.ds(pl.multiple_of(f * 256, 256), 256)]
+
+    def ring_copy(w, up, f):
+        return pltpu.make_async_remote_copy(
+            src_ref=bins_of(blocks, OWN, w, f),
+            dst_ref=bins_of(blocks, ABOVE if up else BELOW, w, f),
+            send_sem=ring_s.at[w, f, up],
+            recv_sem=ring_r.at[w, f, up],
             device_id=before if up else after,
             device_id_type=MESH,
         )
 
-    def sib_copy(w, source, slot):
+    def sib_copy(w, source, slot, f):
         return pltpu.make_async_remote_copy(
-            src_ref=blocks.at[source, w],
-            dst_ref=blocks.at[slot, w],
-            send_sem=sib_s.at[w, slot - X1],
-            recv_sem=sib_r.at[w, slot - X1],
+            src_ref=bins_of(blocks, source, w, f),
+            dst_ref=bins_of(blocks, slot, w, f),
+            send_sem=sib_s.at[w, f, slot - X1],
+            recv_sem=sib_r.at[w, f, slot - X1],
             device_id=sibling,
             device_id_type=MESH,
         )
 
-    def widen(which, source, w):
+    def widen(which, source, w, f):
+        at = pl.ds(pl.multiple_of(f * 256, 256), 256)
+
         def one(i, _):
-            wide[which, w, i] = blocks[source, w, i].astype(F32)
+            wide[which, w, i, :, at] = blocks[source, w, i, :, at].astype(F32)
             return 0
 
-        lax.fori_loop(0, NTM, one, 0)
+        lax.fori_loop(0, NTM, one, 0, unroll=4)
 
     def spread(w):
         for d in range(1, NTM):
             a2a_copy(w, d).wait_recv()
-        ring_copy(w, 1).start()
-        ring_copy(w, 0).start()
-
-        @pl.when(core == 1)
-        def _():
-            sib_copy(w, OWN, X1).start()
-
-        widen(0, OWN, w)
+        for f in range(3):
+
+            @pl.when(jnp.logical_not(first))
+            def _():
+                ring_copy(w, 1, f).start()
+
+            @pl.when(jnp.logical_not(last))
+            def _():
+                ring_copy(w, 0, f).start()
+
+            @pl.when(core == 1)
+            def _():
+                sib_copy(w, OWN, X1, f).start()
+
+        for f in range(3):
+            widen(0, OWN, w, f)
 
     def transform(w, _):
         slot = lax.rem(w, 2)
@@ -281,12 +327,18 @@
 
         lax.fori_loop(0, ROWS // 16, white_rows, 0)
         white = jnp.dot(wh[...], perm[...], preferred_element_type=F32)
-        send[w, :, 0:NB] = white[:ROWS].astype(BF16)
-        send[w, :, NB:] = white[ROWS:].astype(BF16)
-
-        @pl.when(w == 0)
+        for f in range(3):
+            at = f * 256
+            send[w, :, at : at + 128] = white[:ROWS, f * 128 : f * 128 + 128].astype(BF16)
+            send[w, :, at + 128 : at + 256] = white[ROWS:, f * 128 : f * 128 + 128].astype(BF16)
+
+        @pl.when((w == 0) & jnp.logical_not(first | last))
         def _():
             pl.semaphore_wait(barrier, NTM - 1 + 3)
+
+        @pl.when((w == 0) & (first | last))
+        def _():
+            pl.semaphore_wait(barrier, NTM - 1 + 2 + NTM)
 
         for d in range(1, NTM):
             a2a_copy(w, d).start()
@@ -296,105 +348,125 @@
         def _():
             spread(w - 1)
 
+        @pl.when((w > 0) & (first | last))
+        def _():
+            for d in range(NTM):
+                dup_copy(w - 1, d).start()
+
         return 0
 
     lax.fori_loop(0, WL, transform, 0)
 
-    def correlate(k, left, right, w):
-        def bins(i, _):
-            re_at = pl.ds(pl.multiple_of(i * 128, 128), 128)
-            im_at = pl.ds(pl.multiple_of(NB + i * 128, 128), 128)
-            for half in range(2):
-                mine = range(half * 8, half * 8 + 8)
-                start = tuple(acc[k, a, p, :, re_at] for a in mine for p in range(2))
-
-                def window(n, sums):
-                    cr = blocks[right, w, n, :, re_at].astype(F32)
-                    ci = blocks[right, w, n, :, im_at].astype(F32)
-                    new = []
-                    for i, a in enumerate(mine):
-                        ar = wide[left, w, n, a : a + 1, re_at]
-                        ai = wide[left, w, n, a : a + 1, im_at]
-                        new.append(sums[2 * i] + (ar * cr + ai * ci))
-                        new.append(sums[2 * i + 1] + (ai * cr - ar * ci))
-                    return tuple(new)
-
-                sums = lax.fori_loop(0, NTM, window, start)
+    @pl.when(first | last)
+    def _():
+        for d in range(NTM):
+            dup_copy(WL - 1, d).start()
+
+    def correlate(k, left, right, w, f):
+        re_at = pl.ds(pl.multiple_of(f * 256, 128), 128)
+        im_at = pl.ds(pl.multiple_of(f * 256 + 128, 128), 128)
+        at = pl.ds(pl.multiple_of(f * 128, 128), 128)
+        for half in range(2):
+            mine = range(half * 8, half * 8 + 8)
+            start = tuple(acc[k, a, p, :, at] for a in mine for p in range(2))
+
+            def window(n, sums):
+                cr = blocks[right, w, n, :, re_at].astype(F32)
+                ci = blocks[right, w, n, :, im_at].astype(F32)
+                new = []
                 for i, a in enumerate(mine):
-                    for p in range(2):
-                        acc[k, a, p, :, re_at] = sums[2 * i + p]
-            return 0
-
-        lax.fori_loop(0, NB // 128, bins, 0)
-
-    def selfs(w, _):
-        correlate(0, 0, OWN, w)
+                    ar = wide[left, w, n, a : a + 1, re_at]
+                    ai = wide[left, w, n, a : a + 1, im_at]
+                    new.append((sums[2 * i] + ar * cr) + ai * ci)
+                    new.append((sums[2 * i + 1] + ai * cr) - ar * ci)
+                return tuple(new)
+
+            sums = lax.fori_loop(0, NTM, window, start, unroll=8)
+            for i, a in enumerate(mine):
+                for p in range(2):
+                    acc[k, a, p, :, at] = sums[2 * i + p]
+
+    def selfs(i, _):
+        correlate(0, 0, OWN, i // 3, lax.rem(i, 3))
         return 0
 
-    lax.fori_loop(0, WL - 1, selfs, 0)
+    lax.fori_loop(0, 3 * (WL - 1), selfs, 0)
     spread(WL - 1)
-    correlate(0, 0, OWN, WL - 1)
-
-    def give_copy(i):
+    lax.fori_loop(3 * (WL - 1), 3 * WL, selfs, 0)
+
+    def give_copy(i, f):
         return pltpu.make_async_remote_copy(
-            src_ref=give.at[i],
-            dst_ref=take.at[i],
-            send_sem=give_s.at[i],
-            recv_sem=give_r.at[i],
+            src_ref=give.at[i, f],
+            dst_ref=take.at[i, f],
+            send_sem=give_s.at[i, f],
+            recv_sem=give_r.at[i, f],
             device_id=before,
             device_id_type=MESH,
         )
 
-    def hand_over(i, k):
+    def hand_over(i, k, f):
+        at = pl.ds(pl.multiple_of(f * 128, 128), 128)
+
         def one(a, _):
-            give[i, a] = acc[k, a].astype(BF16)
+            give[i, f, a] = acc[k, a, :, :, at].astype(BF16)
             return 0
 
-        lax.fori_loop(0, BS, one, 0)
-        give_copy(i).start()
+        lax.fori_loop(0, BS, one, 0, unroll=4)
+        give_copy(i, f).start()
 
     left3 = core
     right3 = X2 - core
 
-    def partners(w, _):
-        ring_copy(w, 1).wait_recv()
+    def partners(i, _):
+        w = i // 3
+        f = lax.rem(i, 3)
+
+        @pl.when(jnp.logical_not(last))
+        def _():
+            ring_copy(w, 1, f).wait_recv()
+
+        @pl.when(jnp.logical_not(first))
+        def _():
+            ring_copy(w, 0, f).wait_recv()
+
+        @pl.when((first | last) & (f == 0))
+        def _():
+            for d in range(NTM):
+                dup_copy(w, d).wait_recv()
 
         @pl.when(core == 0)
         def _():
-            sib_copy(w, ABOVE, X1).start()
+            sib_copy(w, ABOVE, X1, f).start()
 
         @pl.when(core == 1)
         def _():
-            sib_copy(w, ABOVE, X2).start()
-
-        ring_copy(w, 0).wait_recv()
-        widen(1, BELOW, w)
-        correlate(4, 1, ABOVE, w)
+            sib_copy(w, ABOVE, X2, f).start()
+
+        widen(1, BELOW, w, f)
+        correlate(4, 1, ABOVE, w, f)
 
         @pl.when(w == WL - 1)
         def _():
-            hand_over(0, 4)
-
-        sib_copy(w, OWN, X1).wait_recv()
+            hand_over(0, 4, f)
+
+        correlate(2, 0, ABOVE, w, f)
+        sib_copy(w, OWN, X1, f).wait_recv()
 
         @pl.when(core == 0)
         def _():
-            sib_copy(w, OWN, X2).wait_recv()
-
-        correlate(3, left3, right3, w)
+            sib_copy(w, OWN, X2, f).wait_recv()
+
+        correlate(3, left3, right3, w, f)
 
         @pl.when((w == WL - 1) & (core == 1))
         def _():
-            hand_over(1, 3)
-
-        correlate(1, 0, X1, w)
-        correlate(2, 0, ABOVE, w)
+            hand_over(1, 3, f)
+
+        correlate(1, 0, X1, w, f)
         return 0
 
-    lax.fori_loop(0, WL, partners, 0)
-
-    def out_copy(k):
-        return pltpu.make_async_copy(acc.at[k], out.at[k], out_sem.at[k])
+    def out_copy(k, p):
+        return pltpu.make_async_copy(acc.at[k, :, p], out.at[k, :, :, p], out_sem.at[k, p])
 
     def weight_of(k):
         inside = (block + k < NBLK).astype(F32)
@@ -407,22 +479,28 @@
             acc[k, a] = acc[k, a] * weight
             return 0
 
-        lax.fori_loop(0, BS, one, 0)
-        out_copy(k).start()
+        lax.fori_loop(0, BS, one, 0, unroll=2)
+        for p in range(2):
+            out_copy(k, p).start()
 
     def finish_taken(k, i):
-        give_copy(i).wait_recv()
         weight = weight_of(k)
-
-        def one(a, _):
-            acc[k, a] = take[i, a].astype(F32) * weight
-            return 0
-
-        lax.fori_loop(0, BS, one, 0)
-        out_copy(k).start()
-
-    for k in range(3):
-        finish(k)
+        for f in range(3):
+            give_copy(i, f).wait_recv()
+
+            def one(a, _):
+                acc[k, a, :, :, f * 128 : f * 128 + 128] = take[i, f, a].astype(F32) * weight
+                return 0
+
+            lax.fori_loop(0, BS, one, 0, unroll=4)
+        for p in range(2):
+            out_copy(k, p).start()
+
+    finish(0)
+    lax.fori_loop(0, 3 * WL, partners, 0)
+
+    finish(2)
+    finish(1)
 
     @pl.when(core == 0)
     def _():
@@ -434,32 +512,50 @@
     def _():
         finish_taken(3, 1)
 
-    def drain(w, _):
-        for d in range(1, NTM):
-            a2a_copy(w, d).wait_send()
-        ring_copy(w, 1).wait_send()
-        ring_copy(w, 0).wait_send()
+    def drain(i, _):
+        w = i // 3
+        f = lax.rem(i, 3)
+
+        @pl.when(f == 0)
+        def _():
+            for d in range(1, NTM):
+                a2a_copy(w, d).wait_send()
+
+        @pl.when((first | last) & (f == 0))
+        def _():
+            for d in range(NTM):
+                dup_copy(w, d).wait_send()
+
+        @pl.when(jnp.logical_not(first))
+        def _():
+            ring_copy(w, 1, f).wait_send()
+
+        @pl.when(jnp.logical_not(last))
+        def _():
+            ring_copy(w, 0, f).wait_send()
 
         @pl.when(core == 0)
         def _():
-            sib_copy(w, ABOVE, X1).wait_send()
+            sib_copy(w, ABOVE, X1, f).wait_send()
 
         @pl.when(core == 1)
         def _():
-            sib_copy(w, OWN, X1).wait_send()
-            sib_copy(w, ABOVE, X2).wait_send()
+            sib_copy(w, OWN, X1, f).wait_send()
+            sib_copy(w, ABOVE, X2, f).wait_send()
 
         return 0
 
-    lax.fori_loop(0, WL, drain, 0)
-    give_copy(0).wait_send()
-
-    @pl.when(core == 1)
-    def _():
-        give_copy(1).wait_send()
+    lax.fori_loop(0, 3 * WL, drain, 0)
+    for f in range(3):
+        give_copy(0, f).wait_send()
+
+        @pl.when(core == 1)
+        def _():
+            give_copy(1, f).wait_send()
 
     for k in range(5):
-        out_copy(k).wait()
+        for p in range(2):
+            out_copy(k, p).wait()
 
 
 def body(records, band_gain, pair_mask):
@@ -470,7 +566,7 @@
     dma = pltpu.SemaphoreType.DMA
     sums = pl.pallas_call(
         kernel,
-        out_shape=jax.ShapeDtypeStruct((5, BS, 2, BS, NB), F32),
+        out_shape=jax.ShapeDtypeStruct((5, BS, BS, 2, NB), F32),
         in_specs=[any_space, any_space, vmem, vmem, vmem, vmem, smem],
         out_specs=any_space,
         scratch_shapes=[
@@ -486,19 +582,21 @@
             pltpu.VMEM((5, WL, NTM, BS, 2 * NB), BF16),
             pltpu.VMEM((2, WL, NTM, BS, 2 * NB), F32),
             pltpu.VMEM((5, BS, 2, BS, NB), F32),
-            pltpu.VMEM((2, BS, 2, BS, NB), BF16),
-            pltpu.VMEM((2, BS, 2, BS, NB), BF16),
+            pltpu.VMEM((2, 3, BS, 2, BS, 128), BF16),
+            pltpu.VMEM((2, 3, BS, 2, BS, 128), BF16),
             dma((2,)),
             dma,
             dma((WL, NTM)),
             dma((WL, NTM)),
-            dma((WL, 2)),
-            dma((WL, 2)),
-            dma((WL, 2)),
-            dma((WL, 2)),
-            dma((2,)),
-            dma((2,)),
-            dma((5,)),
+            dma((WL, NTM)),
+            dma((WL, NTM)),
+            dma((WL, 3, 2)),
+            dma((WL, 3, 2)),
+            dma((WL, 3, 2)),
+            dma((WL, 3, 2)),
+            dma((2, 3)),
+            dma((2, 3)),
+            dma((5, 2)),
         ],
         compiler_params=pltpu.CompilerParams(
             collective_id=0, has_side_effects=True, vmem_limit_bytes=58 << 20
@@ -512,10 +610,10 @@
         jnp.asarray(smoother_table()),
         jnp.asarray(order_table()),
         jnp.asarray(hann_row()),
-        band_gain[None, :],
+        band_gain,
         pair_mask,
     )
-    return sums.transpose(0, 1, 3, 2, 4)[None]
+    return sums[None]
 
 
 def solution(mesh):

time: 124 us -> 99.1 us (0.80)
  the two profiles are of different devices: /device:TPU:63 before, /device:TPU:29 now
where the time goes in v1:
time: 99.1 us; the launch traced here: 98.9 us
  Pallas kernels  92.7 us (94%)
  local copies, waits for them, and re-layouts  6.18 us (6%)
    pallas_call x1, Pallas kernels, body(): pl.pallas_call(kernel, out_shape=jax.ShapeDtypeStruct((5, BS, BS, 2, NB),...  92.7 us
    unnamed x1, local copies, waits for them, and re-layouts  6.18 us

profile of v1, /device:TPU:29, one launch (start us, length us, event | category | flops | bytes accessed | tf_op | source)
XLA Modules:
  0.0 98.9 jit_solution(15575270801716816918)
XLA Ops:
  0.0 92.7 %shard_map.73 = f32[5,16,16,2,384]{4,3,2,1,0:T(2,128)} custom-call(f32[4,256,4096]{2,1,0:T(8,128)} %bitcast.3, bf16[2,3072,512]{2,1,0:T(8,128)(2,1)} %constant.8.clone.tab_hbm, bf16[512,512]{1,0:T(8,128)(2,1)} %constant.9.clone.smooth, bf16[512,384]{1,0:T(8,128)(2,1)} %constant.10.clone.perm, f32[1,4096]{1,0:T(1,128)} %constant.11.clone.hann, f32[384]{0:T(512)} %gain.1, ...), custom_call_target="tpu_custom_call" | custom-call | flops 10000000000 | bytes 30000000 | tf_op jit(solution)/shard_map/pallas_call | solution.py:567
  92.7 6.2 %copy.9 = f32[1,5,16,16,2,384]{5,4,3,2,1,0:T(2,128)} copy(f32[1,5,16,16,2,384]{5,4,3,2,1,0:T(2,128)} %bitcast.2) | data formatting | bytes 7864320

commit v2 on v1

--- a/solution.py
+++ b/solution.py
@@ -466,7 +466,7 @@
         return 0
 
     def out_copy(k, p):
-        return pltpu.make_async_copy(acc.at[k, :, p], out.at[k, :, :, p], out_sem.at[k, p])
+        return pltpu.make_async_copy(acc.at[k, :, p], out.at[k, :, p], out_sem.at[k, p])
 
     def weight_of(k):
         inside = (block + k < NBLK).astype(F32)
@@ -556,6 +556,24 @@
     for k in range(5):
         for p in range(2):
             out_copy(k, p).wait()
+
+
+def place_kernel(sums, out, held, in_sem, out_sem):
+    def take_in(k):
+        return pltpu.make_async_copy(sums.at[k], held.at[k], in_sem.at[k])
+
+    def put_out(k, p):
+        return pltpu.make_async_copy(held.at[k, :, p], out.at[k, :, :, p], out_sem.at[k, p])
+
+    for k in range(5):
+        take_in(k).start()
+    for k in range(5):
+        take_in(k).wait()
+        for p in range(2):
+            put_out(k, p).start()
+    for k in range(5):
+        for p in range(2):
+            put_out(k, p).wait()
 
 
 def body(records, band_gain, pair_mask):
@@ -566,7 +584,7 @@
     dma = pltpu.SemaphoreType.DMA
     sums = pl.pallas_call(
         kernel,
-        out_shape=jax.ShapeDtypeStruct((5, BS, BS, 2, NB), F32),
+        out_shape=jax.ShapeDtypeStruct((5, BS, 2, BS, NB), F32),
         in_specs=[any_space, any_space, vmem, vmem, vmem, vmem, smem],
         out_specs=any_space,
         scratch_shapes=[
@@ -613,7 +631,15 @@
         band_gain,
         pair_mask,
     )
-    return sums[None]
+    stacks = pl.pallas_call(
+        place_kernel,
+        out_shape=jax.ShapeDtypeStruct((5, BS, BS, 2, NB), F32),
+        in_specs=[any_space],
+        out_specs=any_space,
+        scratch_shapes=[pltpu.VMEM((5, BS, 2, BS, NB), F32), dma((5,)), dma((5, 2))],
+        cost_estimate=pl.CostEstimate(flops=0, bytes_accessed=8 * 10**6, transcendentals=0),
+    )(sums)
+    return stacks[None]
 
 
 def solution(mesh):

time: 99.1 us -> 96 us (0.969)
  local copies, waits for them, and re-layouts: 6.18 us -> 0 us
  Pallas kernels: 92.7 us -> 95.9 us
    unnamed x1 -> x0, local copies, waits for them, and re-layouts: 6.18 us -> none
    pallas_call x1 -> x2, Pallas kernels: 92.7 us -> 95.9 us  [the longest x1 92.7 us: body(): pl.pallas_call(kernel, out_shape=jax.ShapeDtypeStruct((5, BS, 2, BS, NB),...]
where the time goes in v2:
time: 96 us; the launch traced here: 95.9 us
  Pallas kernels  95.9 us (100%)
    pallas_call x1, Pallas kernels, body(): pl.pallas_call(kernel, out_shape=jax.ShapeDtypeStruct((5, BS, 2, BS, NB),...  92.7 us
    pallas_call x1, Pallas kernels, body(): pl.pallas_call(place_kernel, out_shape=jax.ShapeDtypeStruct((5, BS, BS, 2...  3.17 us

profile of v2, /device:TPU:29, one launch (start us, length us, event | category | flops | bytes accessed | tf_op | source)
XLA Modules:
  0.0 95.9 jit_solution(11368105014836186924)
XLA Ops:
  0.0 92.7 %shard_map.73.sums = f32[5,16,2,16,384]{4,3,2,1,0:T(8,128)} custom-call(f32[4,256,4096]{2,1,0:T(8,128)} %bitcast.2, bf16[2,3072,512]{2,1,0:T(8,128)(2,1)} %constant.8.clone.tab_hbm, bf16[512,512]{1,0:T(8,128)(2,1)} %constant.9.clone.smooth, bf16[512,384]{1,0:T(8,128)(2,1)} %constant.10.clone.perm, f32[1,4096]{1,0:T(1,128)} %constant.11.clone.hann, f32[384]{0:T(512)} %gain.1, ...), custom_call_target="tpu_custom_call" | custom-call | flops 10000000000 | bytes 30000000 | tf_op jit(solution)/shard_map/pallas_call | solution.py:585
  92.7 3.2 %shard_map.74 = f32[5,16,16,2,384]{4,3,2,1,0:T(2,128)} custom-call(f32[5,16,2,16,384]{4,3,2,1,0:T(8,128)} %shard_map.73.sums), custom_call_target="tpu_custom_call" | custom-call | bytes 8000000 | tf_op jit(solution)/shard_map/pallas_call | solution.py:634

commit v3 on v2

--- a/solution.py
+++ b/solution.py
@@ -93,6 +93,7 @@
     send,
     blocks,
     wide,
+    other,
     acc,
     give,
     take,
@@ -218,9 +219,21 @@
 
     def widen(which, source, w, f):
         at = pl.ds(pl.multiple_of(f * 256, 256), 256)
+        to = pl.multiple_of(f * 384, 384)
 
         def one(i, _):
-            wide[which, w, i, :, at] = blocks[source, w, i, :, at].astype(F32)
+            both = blocks[source, w, i, :, at].astype(F32)
+            wide[which, w, i, :, pl.ds(to, 256)] = both
+            wide[which, w, i, :, pl.ds(to + 256, 128)] = both[:, :128] + both[:, 128:]
+            return 0
+
+        lax.fori_loop(0, NTM, one, 0, unroll=4)
+
+    def widen_other(slot, w, f):
+        at = pl.ds(pl.multiple_of(f * 256, 256), 256)
+
+        def one(i, _):
+            other[slot - ABOVE, i] = blocks[slot, w, i, :, at].astype(F32)
             return 0
 
         lax.fori_loop(0, NTM, one, 0, unroll=4)
@@ -363,31 +376,36 @@
             dup_copy(WL - 1, d).start()
 
     def correlate(k, left, right, w, f):
-        re_at = pl.ds(pl.multiple_of(f * 256, 128), 128)
-        im_at = pl.ds(pl.multiple_of(f * 256 + 128, 128), 128)
+        re_at = pl.ds(pl.multiple_of(f * 384, 128), 128)
+        im_at = pl.ds(pl.multiple_of(f * 384 + 128, 128), 128)
+        sum_at = pl.ds(pl.multiple_of(f * 384 + 256, 128), 128)
         at = pl.ds(pl.multiple_of(f * 128, 128), 128)
-        for half in range(2):
-            mine = range(half * 8, half * 8 + 8)
-            start = tuple(acc[k, a, p, :, at] for a in mine for p in range(2))
+        zero = jnp.zeros((BS, 128), F32)
+        for part in range(4):
+            mine = range(part * 4, part * 4 + 4)
 
             def window(n, sums):
-                cr = blocks[right, w, n, :, re_at].astype(F32)
-                ci = blocks[right, w, n, :, im_at].astype(F32)
+                if right is None:
+                    cr = wide[0, w, n, :, re_at]
+                    ci = wide[0, w, n, :, im_at]
+                else:
+                    cr = other[right, n, :, :128]
+                    ci = other[right, n, :, 128:]
+                plus, minus = cr + ci, cr - ci
                 new = []
                 for i, a in enumerate(mine):
-                    ar = wide[left, w, n, a : a + 1, re_at]
-                    ai = wide[left, w, n, a : a + 1, im_at]
-                    new.append((sums[2 * i] + ar * cr) + ai * ci)
-                    new.append((sums[2 * i + 1] + ai * cr) - ar * ci)
+                    new.append(sums[3 * i] + wide[left, w, n, a : a + 1, sum_at] * cr)
+                    new.append(sums[3 * i + 1] + wide[left, w, n, a : a + 1, re_at] * plus)
+                    new.append(sums[3 * i + 2] + wide[left, w, n, a : a + 1, im_at] * minus)
                 return tuple(new)
 
-            sums = lax.fori_loop(0, NTM, window, start, unroll=8)
+            sums = lax.fori_loop(0, NTM, window, (zero,) * 12, unroll=8)
             for i, a in enumerate(mine):
-                for p in range(2):
-                    acc[k, a, p, :, at] = sums[2 * i + p]
+                acc[k, a, 0, :, at] += sums[3 * i] - sums[3 * i + 2]
+                acc[k, a, 1, :, at] += sums[3 * i] - sums[3 * i + 1]
 
     def selfs(i, _):
-        correlate(0, 0, OWN, i // 3, lax.rem(i, 3))
+        correlate(0, 0, None, i // 3, lax.rem(i, 3))
         return 0
 
     lax.fori_loop(0, 3 * (WL - 1), selfs, 0)
@@ -415,9 +433,9 @@
         give_copy(i, f).start()
 
     left3 = core
-    right3 = X2 - core
-
-    def partners(i, _):
+    right3 = X2 - core - ABOVE
+
+    def arrive(i):
         w = i // 3
         f = lax.rem(i, 3)
 
@@ -443,18 +461,25 @@
             sib_copy(w, ABOVE, X2, f).start()
 
         widen(1, BELOW, w, f)
-        correlate(4, 1, ABOVE, w, f)
+        widen_other(ABOVE, w, f)
+        correlate(4, 1, ABOVE - ABOVE, w, f)
 
         @pl.when(w == WL - 1)
         def _():
             hand_over(0, 4, f)
 
-        correlate(2, 0, ABOVE, w, f)
+        correlate(2, 0, ABOVE - ABOVE, w, f)
+
+    def use_shared(i):
+        w = i // 3
+        f = lax.rem(i, 3)
         sib_copy(w, OWN, X1, f).wait_recv()
+        widen_other(X1, w, f)
 
         @pl.when(core == 0)
         def _():
             sib_copy(w, OWN, X2, f).wait_recv()
+            widen_other(X2, w, f)
 
         correlate(3, left3, right3, w, f)
 
@@ -462,7 +487,17 @@
         def _():
             hand_over(1, 3, f)
 
-        correlate(1, 0, X1, w, f)
+        correlate(1, 0, X1 - ABOVE, w, f)
+
+    def partners(i, _):
+        @pl.when(i < 3 * WL)
+        def _():
+            arrive(i)
+
+        @pl.when(i > 0)
+        def _():
+            use_shared(i - 1)
+
         return 0
 
     def out_copy(k, p):
@@ -497,7 +532,7 @@
             out_copy(k, p).start()
 
     finish(0)
-    lax.fori_loop(0, 3 * WL, partners, 0)
+    lax.fori_loop(0, 3 * WL + 1, partners, 0)
 
     finish(2)
     finish(1)
@@ -598,7 +633,8 @@
             pltpu.VMEM((16, EXT), F32),
             pltpu.VMEM((WL, ROWS, 2 * NB), BF16),
             pltpu.VMEM((5, WL, NTM, BS, 2 * NB), BF16),
-            pltpu.VMEM((2, WL, NTM, BS, 2 * NB), F32),
+            pltpu.VMEM((2, WL, NTM, BS, 3 * NB), F32),
+            pltpu.VMEM((3, NTM, BS, 256), F32),
             pltpu.VMEM((5, BS, 2, BS, NB), F32),
             pltpu.VMEM((2, 3, BS, 2, BS, 128), BF16),
             pltpu.VMEM((2, 3, BS, 2, BS, 128), BF16),

time: 96 us -> 92.2 us (0.960)
  Pallas kernels: 95.9 us -> 92.1 us
    pallas_call x1, Pallas kernels: 92.7 us -> 88.9 us  [body(): pl.pallas_call(kernel, out_shape=jax.ShapeDtypeStruct((5, BS, 2, BS, NB),...]
where the time goes in v3:
time: 92.2 us; the launch traced here: 92.1 us
  Pallas kernels  92.1 us (100%)
    pallas_call x1, Pallas kernels, body(): pl.pallas_call(kernel, out_shape=jax.ShapeDtypeStruct((5, BS, 2, BS, NB),...  88.9 us
    pallas_call x1, Pallas kernels, body(): pl.pallas_call(place_kernel, out_shape=jax.ShapeDtypeStruct((5, BS, BS, 2...  3.17 us

profile of v3, /device:TPU:29, one launch (start us, length us, event | category | flops | bytes accessed | tf_op | source)
XLA Modules:
  0.0 92.1 jit_solution(8525085743133546566)
XLA Ops:
  0.0 88.9 %shard_map.73.sums = f32[5,16,2,16,384]{4,3,2,1,0:T(8,128)} custom-call(f32[4,256,4096]{2,1,0:T(8,128)} %bitcast.2, bf16[2,3072,512]{2,1,0:T(8,128)(2,1)} %constant.8.clone.tab_hbm, bf16[512,512]{1,0:T(8,128)(2,1)} %constant.9.clone.smooth, bf16[512,384]{1,0:T(8,128)(2,1)} %constant.10.clone.perm, f32[1,4096]{1,0:T(1,128)} %constant.11.clone.hann, f32[384]{0:T(512)} %gain.1, ...), custom_call_target="tpu_custom_call" | custom-call | flops 10000000000 | bytes 30000000 | tf_op jit(solution)/shard_map/pallas_call | solution.py:620
  88.9 3.2 %shard_map.74 = f32[5,16,16,2,384]{4,3,2,1,0:T(2,128)} custom-call(f32[5,16,2,16,384]{4,3,2,1,0:T(8,128)} %shard_map.73.sums), custom_call_target="tpu_custom_call" | custom-call | bytes 8000000 | tf_op jit(solution)/shard_map/pallas_call | solution.py:670

commit v4 on v3

--- a/solution.py
+++ b/solution.py
@@ -357,14 +357,14 @@
             a2a_copy(w, d).start()
         blocks[OWN, w, t] = send[w, pl.ds(pl.multiple_of(t * BS, BS), BS)]
 
-        @pl.when(w > 0)
-        def _():
-            spread(w - 1)
-
         @pl.when((w > 0) & (first | last))
         def _():
             for d in range(NTM):
                 dup_copy(w - 1, d).start()
+
+        @pl.when(w > 0)
+        def _():
+            spread(w - 1)
 
         return 0
 

time: 92.2 us -> 89.6 us (0.972); the launches traced: 92.1 us -> 88.1 us
  Pallas kernels: 92.1 us -> 88.1 us
    pallas_call x1, Pallas kernels: 88.9 us -> 84.9 us  [body(): pl.pallas_call(kernel, out_shape=jax.ShapeDtypeStruct((5, BS, 2, BS, NB),...]
where the time goes in v4:
time: 89.6 us; the launch traced here: 88.1 us
  Pallas kernels  88.1 us (98%)
    pallas_call x1, Pallas kernels, body(): pl.pallas_call(kernel, out_shape=jax.ShapeDtypeStruct((5, BS, 2, BS, NB),...  84.9 us
    pallas_call x1, Pallas kernels, body(): pl.pallas_call(place_kernel, out_shape=jax.ShapeDtypeStruct((5, BS, BS, 2...  3.17 us

profile of v4, /device:TPU:29, one launch (start us, length us, event | category | flops | bytes accessed | tf_op | source)
XLA Modules:
  0.0 88.1 jit_solution(6460902167571126976)
XLA Ops:
  0.0 84.9 %shard_map.73.sums = f32[5,16,2,16,384]{4,3,2,1,0:T(8,128)} custom-call(f32[4,256,4096]{2,1,0:T(8,128)} %bitcast.2, bf16[2,3072,512]{2,1,0:T(8,128)(2,1)} %constant.8.clone.tab_hbm, bf16[512,512]{1,0:T(8,128)(2,1)} %constant.9.clone.smooth, bf16[512,384]{1,0:T(8,128)(2,1)} %constant.10.clone.perm, f32[1,4096]{1,0:T(1,128)} %constant.11.clone.hann, f32[384]{0:T(512)} %gain.1, ...), custom_call_target="tpu_custom_call" | custom-call | flops 10000000000 | bytes 30000000 | tf_op jit(solution)/shard_map/pallas_call | solution.py:620
  84.9 3.2 %shard_map.74 = f32[5,16,16,2,384]{4,3,2,1,0:T(2,128)} custom-call(f32[5,16,2,16,384]{4,3,2,1,0:T(8,128)} %shard_map.73.sums), custom_call_target="tpu_custom_call" | custom-call | bytes 8000000 | tf_op jit(solution)/shard_map/pallas_call | solution.py:670

commit v5 on v4

--- a/solution.py
+++ b/solution.py
@@ -408,9 +408,9 @@
         correlate(0, 0, None, i // 3, lax.rem(i, 3))
         return 0
 
-    lax.fori_loop(0, 3 * (WL - 1), selfs, 0)
+    lax.fori_loop(0, 5, selfs, 0)
     spread(WL - 1)
-    lax.fori_loop(3 * (WL - 1), 3 * WL, selfs, 0)
+    lax.fori_loop(5, 3 * WL, selfs, 0)
 
     def give_copy(i, f):
         return pltpu.make_async_remote_copy(

time: 89.6 us -> 91.7 us (1.023)
  Pallas kernels: 88.1 us -> 90.4 us
    pallas_call x1, Pallas kernels: 84.9 us -> 87.2 us  [body(): pl.pallas_call(kernel, out_shape=jax.ShapeDtypeStruct((5, BS, 2, BS, NB),...]
where the time goes in v5:
time: 91.7 us; the launch traced here: 90.4 us
  Pallas kernels  90.4 us (99%)
    pallas_call x1, Pallas kernels, body(): pl.pallas_call(kernel, out_shape=jax.ShapeDtypeStruct((5, BS, 2, BS, NB),...  87.2 us
    pallas_call x1, Pallas kernels, body(): pl.pallas_call(place_kernel, out_shape=jax.ShapeDtypeStruct((5, BS, BS, 2...  3.17 us

profile of v5, /device:TPU:29, one launch (start us, length us, event | category | flops | bytes accessed | tf_op | source)
XLA Modules:
  0.0 90.4 jit_solution(2913344662480828058)
XLA Ops:
  0.0 87.2 %shard_map.73.sums = f32[5,16,2,16,384]{4,3,2,1,0:T(8,128)} custom-call(f32[4,256,4096]{2,1,0:T(8,128)} %bitcast.2, bf16[2,3072,512]{2,1,0:T(8,128)(2,1)} %constant.8.clone.tab_hbm, bf16[512,512]{1,0:T(8,128)(2,1)} %constant.9.clone.smooth, bf16[512,384]{1,0:T(8,128)(2,1)} %constant.10.clone.perm, f32[1,4096]{1,0:T(1,128)} %constant.11.clone.hann, f32[384]{0:T(512)} %gain.1, ...), custom_call_target="tpu_custom_call" | custom-call | flops 10000000000 | bytes 30000000 | tf_op jit(solution)/shard_map/pallas_call | solution.py:620
  87.2 3.2 %shard_map.74 = f32[5,16,16,2,384]{4,3,2,1,0:T(2,128)} custom-call(f32[5,16,2,16,384]{4,3,2,1,0:T(8,128)} %shard_map.73.sums), custom_call_target="tpu_custom_call" | custom-call | bytes 8000000 | tf_op jit(solution)/shard_map/pallas_call | solution.py:670

commit v6 on v4

--- a/solution.py
+++ b/solution.py
@@ -229,11 +229,11 @@
 
         lax.fori_loop(0, NTM, one, 0, unroll=4)
 
-    def widen_other(slot, w, f):
+    def widen_other(slot, to, w, f):
         at = pl.ds(pl.multiple_of(f * 256, 256), 256)
 
         def one(i, _):
-            other[slot - ABOVE, i] = blocks[slot, w, i, :, at].astype(F32)
+            other[to, i] = blocks[slot, w, i, :, at].astype(F32)
             return 0
 
         lax.fori_loop(0, NTM, one, 0, unroll=4)
@@ -461,25 +461,25 @@
             sib_copy(w, ABOVE, X2, f).start()
 
         widen(1, BELOW, w, f)
-        widen_other(ABOVE, w, f)
-        correlate(4, 1, ABOVE - ABOVE, w, f)
+        above = 3 * lax.rem(i, 2)
+        widen_other(ABOVE, above, w, f)
+        correlate(4, 1, above, w, f)
 
         @pl.when(w == WL - 1)
         def _():
             hand_over(0, 4, f)
 
-        correlate(2, 0, ABOVE - ABOVE, w, f)
 
     def use_shared(i):
         w = i // 3
         f = lax.rem(i, 3)
         sib_copy(w, OWN, X1, f).wait_recv()
-        widen_other(X1, w, f)
+        widen_other(X1, 1, w, f)
 
         @pl.when(core == 0)
         def _():
             sib_copy(w, OWN, X2, f).wait_recv()
-            widen_other(X2, w, f)
+            widen_other(X2, 2, w, f)
 
         correlate(3, left3, right3, w, f)
 
@@ -487,7 +487,8 @@
         def _():
             hand_over(1, 3, f)
 
-        correlate(1, 0, X1 - ABOVE, w, f)
+        correlate(1, 0, 1, w, f)
+        correlate(2, 0, 3 * lax.rem(i, 2), w, f)
 
     def partners(i, _):
         @pl.when(i < 3 * WL)
@@ -634,7 +635,7 @@
             pltpu.VMEM((WL, ROWS, 2 * NB), BF16),
             pltpu.VMEM((5, WL, NTM, BS, 2 * NB), BF16),
             pltpu.VMEM((2, WL, NTM, BS, 3 * NB), F32),
-            pltpu.VMEM((3, NTM, BS, 256), F32),
+            pltpu.VMEM((4, NTM, BS, 256), F32),
             pltpu.VMEM((5, BS, 2, BS, NB), F32),
             pltpu.VMEM((2, 3, BS, 2, BS, 128), BF16),
             pltpu.VMEM((2, 3, BS, 2, BS, 128), BF16),

time: 89.6 us -> 89.5 us (level)
  no operation moved by 1% of the time
where the time goes in v6:
time: 89.5 us; the launch traced here: 87.9 us
  Pallas kernels  87.9 us (98%)
    pallas_call x1, Pallas kernels, body(): pl.pallas_call(kernel, out_shape=jax.ShapeDtypeStruct((5, BS, 2, BS, NB),...  84.7 us
    pallas_call x1, Pallas kernels, body(): pl.pallas_call(place_kernel, out_shape=jax.ShapeDtypeStruct((5, BS, BS, 2...  3.17 us

profile of v6, /device:TPU:29, one launch (start us, length us, event | category | flops | bytes accessed | tf_op | source)
XLA Modules:
  0.0 87.9 jit_solution(13820806486726754619)
XLA Ops:
  0.0 84.7 %shard_map.73.sums = f32[5,16,2,16,384]{4,3,2,1,0:T(8,128)} custom-call(f32[4,256,4096]{2,1,0:T(8,128)} %bitcast.2, bf16[2,3072,512]{2,1,0:T(8,128)(2,1)} %constant.8.clone.tab_hbm, bf16[512,512]{1,0:T(8,128)(2,1)} %constant.9.clone.smooth, bf16[512,384]{1,0:T(8,128)(2,1)} %constant.10.clone.perm, f32[1,4096]{1,0:T(1,128)} %constant.11.clone.hann, f32[384]{0:T(512)} %gain.1, ...), custom_call_target="tpu_custom_call" | custom-call | flops 10000000000 | bytes 30000000 | tf_op jit(solution)/shard_map/pallas_call | solution.py:621
  84.7 3.2 %shard_map.74 = f32[5,16,16,2,384]{4,3,2,1,0:T(2,128)} custom-call(f32[5,16,2,16,384]{4,3,2,1,0:T(8,128)} %shard_map.73.sums), custom_call_target="tpu_custom_call" | custom-call | bytes 8000000 | tf_op jit(solution)/shard_map/pallas_call | solution.py:671
